TPU v7x, 256 devices: a whole 4x4x8 slice. The times are simulated.
256 devices in a mesh: section: 8 (over z), tensor: 4 (over y), dp: 8 (over x, core).
Axes of the slice: x: 4, y: 4, z: 8, core: 2. Of those that a mesh axis runs over, the one named last changes fastest.
Arguments:
- hidden: bfloat16 [896, 5376], P('dp', ('section', 'tensor')), may hold values from -6 to 6
- head_weight: bfloat16 [5376, 131072], P(None, ('section', 'tensor', 'dp')), may hold values from -0.24549513 to 0.24549513
- targets: int32 [896], replicated, may hold values from 0 to 131071
- response_mask: int32 [896], replicated, may hold values from 0 to 1, as said below
- pair_ids: int32 [16], replicated, may hold values from 0 to 7, as said below
- ref_logprobs: float32 [16], replicated, may hold values from -3 to 3
Outputs:
- logprobs: float32 [16], replicated
- grad_hidden: bfloat16 [896, 5376], P('dp', ('section', 'tensor'))
- grad_weight: bfloat16 [5376, 131072], P(None, ('section', 'tensor', 'dp'))
Inputs may be any that keep to these rules, and one draw needn't show every extreme that they name: `pair_ids`: each pair id 0 to 7 names exactly two sequences. `response_mask`: in each sequence the ones form a suffix of at least 28 positions.
All inputs are finite; a program needn't handle non-finite values.
Results may differ from a plain program's by a relative error of at most 0.0046.
Values may be sent and summed in bfloat16 or wider, within the bound.
A program may use at most 128 MiB of HBM per device.

v0:
```python
import heapq
import itertools
import math

import jax
import jax.numpy as jnp
from jax import lax
from jax.experimental import pallas as pl
from jax.experimental.pallas import tpu as pltpu
from jax.sharding import PartitionSpec as P

loss_scale = 2048.0
beta_value = 2.0

MESH = pl.DeviceIdType.MESH
SIZE = {"z": 8, "y": 4, "x": 4}
BLOB = 11
CUTS = ((0, 4), (4, 8), (8, 11))
LANES = 128
TILE = 16
ROWS = 112
WIDE = 168
TOK = 896
SEQS = 16
SEQ = 56
COLS = 512
PAIRS = 16
PAIR = 336
PADDED = 384
F32 = jnp.float32
BF16 = jnp.bfloat16
ISSUE_US = 0.05
HOP_US = 1.5
EACH_HOP_US = 0.5
LINK = 45.0e3
CORE_LINK = 600.0e3
MATMUL_US = 0.8
ADD_US = 0.06
FAR_FIRST = (4, 3, -3, 2, -2, 1, -1, 0)


class Comm:
    def __init__(self, send_sem, recv_sem):
        self.z = lax.axis_index("section")
        self.y = lax.axis_index("tensor")
        dp = lax.axis_index("dp")
        self.dp = dp
        self.x = dp // 2
        self.c = lax.rem(dp, 2)
        self.send_sem, self.recv_sem = send_sem, recv_sem
        self.used = 0
        self.unsent = []
        self.line = Timeline()

    def at(self, axis):
        return {"z": self.z, "y": self.y, "x": self.x}[axis]

    def step(self, axis, offset):
        return lax.rem(self.at(axis) + offset + 2 * SIZE[axis], SIZE[axis])

    def device(self, axis, offset):
        z, y, x = self.z, self.y, self.x
        position = self.step(axis, offset)
        if axis == "z":
            z = position
        elif axis == "y":
            y = position
        else:
            x = position
        return (z, y, 2 * x + self.c)

    def sibling(self):
        return (self.z, self.y, 2 * self.x + 1 - self.c)

    def partner(self):
        return (self.z, self.y + 1 - 2 * lax.rem(self.y, 2), self.dp)

    def send(self, src, dst, axis, offset=None, landing=None):
        i = self.used
        self.used += 1
        if offset is None:
            device = axis
        else:
            device = self.sibling() if axis == "c" else self.device(axis, offset)
        copy = pltpu.make_async_remote_copy(
            src_ref=src,
            dst_ref=dst,
            send_sem=self.send_sem.at[i],
            recv_sem=self.recv_sem.at[i],
            device_id=device,
            device_id_type=MESH,
        )
        copy.start()
        self.unsent.append(copy)
        land = dst if landing is None else landing
        back = pltpu.make_async_remote_copy(
            src_ref=land,
            dst_ref=land,
            send_sem=self.send_sem.at[i],
            recv_sem=self.recv_sem.at[i],
            device_id=device,
            device_id_type=MESH,
        )
        size = math.prod(src.shape) * jnp.dtype(src.dtype).itemsize
        return Landing(self.line, back, self.line.now if offset is None else self.line.carry(axis, offset, size))

    def drain(self):
        for copy in self.unsent:
            copy.wait_send()
        self.unsent = []


class Event:
    def __init__(self):
        self.fired = False
        self.waiting = []


class Landing:
    def __init__(self, line, copy, when):
        self.line, self.copy, self.when = line, copy, when

    def __call__(self):
        self.copy.wait_recv()
        self.line.now = max(self.line.now, self.when)


class Timeline:
    def __init__(self):
        self.now = 0.0
        self.heap = []
        self.order = itertools.count()
        self.work = []
        self.free = {}

    def spawn(self, generator, when=0.0):
        heapq.heappush(self.heap, (max(self.now, when), next(self.order), generator))

    def fire(self, event):
        event.fired = True
        for generator in event.waiting:
            self.spawn(generator)
        event.waiting = []

    def busy(self, us):
        self.now += us

    def carry(self, axis, offset, size):
        self.busy(ISSUE_US)
        link = (axis, offset > 0)
        hops = 1 if axis == "c" else abs(offset)
        us = size / CORE_LINK if axis == "c" else hops * size / LINK
        end = max(self.now, self.free.get(link, 0.0)) + us
        self.free[link] = end
        return end + HOP_US + (EACH_HOP_US * (hops + 1) if axis != "c" else EACH_HOP_US)

    def run(self):
        while self.heap:
            while self.work and self.heap[0][0] > self.now + 0.4 * MATMUL_US:
                self.work.pop(0)()
                self.busy(MATMUL_US)
            when, _, generator = heapq.heappop(self.heap)
            self.now = max(self.now, when)
            while True:
                try:
                    wish = next(generator)
                except StopIteration:
                    break
                if isinstance(wish, Event):
                    if wish.fired:
                        continue
                    wish.waiting.append(generator)
                else:
                    self.spawn(generator, max([landing.when for landing in wish], default=0.0))
                break
        while self.work:
            self.work.pop(0)()
            self.busy(MATMUL_US)


NEAR_FIRST = (1, -1, 2, -2, 3, -3, 4)


def ring_views(comm, array):
    core = comm.c
    (l0, h0), (l1, h1), _ = CUTS

    def cut(lo, hi, half):
        middle = (lo + hi) // 2
        return slice(lo, hi) if half is None else slice(lo, middle) if half == 0 else slice(middle, hi)

    def some(half):
        return slice(None) if half is None else pl.ds(2 * half, 2)

    return (
        (
            ("y", lambda z, y, half=None: array.at[z, y, comm.x, core, cut(l0, h0, half)]),
            ("x", lambda z, x, half=None: array.at[z, some(half), x, core, l0:h0]),
        ),
        (
            ("x", lambda z, x, half=None: array.at[z, comm.y, x, core, cut(l1, h1, half)]),
            ("y", lambda z, y, half=None: array.at[z, y, some(half), core, l1:h1]),
        ),
    )


def third_view(comm, array):
    lo, hi = CUTS[2]

    def view(z, y, half=None):
        return array.at[z, y, slice(None) if half is None else pl.ds(2 * half, 2), comm.c, lo:hi]

    return view


def gather(comm, held, line, add_logits):
    place = (comm.z, comm.y, comm.x, comm.c)
    missing = {d: 6 for d in FAR_FIRST}

    def finish(d):
        missing[d] -= 1
        if missing[d] == 0:
            z = comm.step("z", d)
            src = held.at[z, :, :, comm.c]
            wait = comm.send(src, src, "c", 1, landing=held.at[z, :, :, 1 - comm.c])

            def rest():
                yield [wait]
                wait()
                add_logits(z, d)
                line.busy(MATMUL_US)

            line.spawn(rest())

    def ring(axis, view, d):
        z = comm.step("z", d)
        src = view(z, comm.at(axis))
        left = comm.send(src, src, axis, 1, landing=view(z, comm.step(axis, -1)))
        right = comm.send(src, src, axis, -1, landing=view(z, comm.step(axis, 1)))
        yield [left]
        left()
        src = view(z, comm.step(axis, -1), 0)
        left = comm.send(src, src, axis, 1, landing=view(z, comm.step(axis, 2), 0))
        yield [right]
        right()
        src = view(z, comm.step(axis, 1), 1)
        right = comm.send(src, src, axis, -1, landing=view(z, comm.step(axis, 2), 1))
        yield [left, right]
        left()
        right()

    def chain(rings, d, wait=None):
        if wait is not None:
            yield [wait]
            wait()
        for axis, view in rings:
            yield from ring(axis, view, d)
        finish(d)

    views = ring_views(comm, held)
    first = slice(CUTS[0][0], CUTS[1][1])

    def arrive(d, wait):
        yield [wait]
        wait()
        for rings in views:
            line.spawn(chain(rings, d))

    def along_z(y):
        third = third_view(comm, held)
        for s in (1, 2, 3, 4):
            h0, h1 = (0, 1) if s == 4 else (None, None)
            src = third(comm.step("z", 1 - s), y, h0)
            left = comm.send(src, src, "z", 1, landing=third(comm.step("z", -s), y, h0))
            src = third(comm.step("z", s - 1), y, h1)
            right = comm.send(src, src, "z", -1, landing=third(comm.step("z", s), y, h1))
            if s == 1:
                finish(0)
            yield [left, right]
            left()
            right()
            if s < 4:
                finish(-s)
                finish(s)
        finish(4)

    def start_third():
        lo, hi = CUTS[2]
        src = held.at[(*place, slice(lo, hi))]
        waits = [
            comm.send(
                src, src, "x", o, landing=held.at[comm.z, comm.y, comm.step("x", -o), comm.c, lo:hi]
            )
            for o in (1, -1, 2)
        ]
        yield waits
        for wait in waits:
            wait()
        third = third_view(comm, held)
        src = third(comm.z, comm.y)
        waits = [
            comm.send(src, src, "y", o, landing=third(comm.z, comm.step("y", -o))) for o in (1, -1, 2)
        ]
        line.spawn(along_z(comm.y))
        for wait, o in zip(waits, (1, -1, 2)):
            yield [wait]
            wait()
            line.spawn(along_z(comm.step("y", -o)))

    line.spawn(start_third())
    for rings in views:
        line.spawn(chain(rings, 0))

    def spread():
        src = held.at[(*place, first)]
        for o in NEAR_FIRST:
            landing = held.at[comm.step("z", -o), comm.y, comm.x, comm.c, first]
            wait = comm.send(src, src, "z", o, landing=landing)
            line.spawn(arrive(4 if o == 4 else -o, wait))
        return
        yield

    line.spawn(spread())
    line.run()


def reduce_shapes():
    t0, t1, t2 = (hi - lo for lo, hi in CUTS)
    end = (TILE, LANES)
    shapes = []
    for tiles in (t0, t1):
        shapes += [
            pltpu.VMEM((8, 2, 2, tiles, *end), BF16),
            pltpu.VMEM((8, 2, 4, tiles, *end), BF16),
            pltpu.VMEM((8, 2, tiles // 2, *end), BF16),
            pltpu.VMEM((8, 2, tiles, *end), BF16),
            pltpu.VMEM((7, tiles, *end), BF16),
        ]
    shapes += [
        pltpu.VMEM((4, 2, 2, t2, *end), BF16),
        pltpu.VMEM((4, 3, 2, 4, t2, *end), BF16),
        pltpu.VMEM((3, 4, t2, *end), BF16),
        pltpu.VMEM((4, t2, *end), F32),
        pltpu.VMEM((3, t2, *end), F32),
    ]
    return shapes


def reduce(comm, partial, result, buffers, line, ready):
    def add(own, *others):
        if len(others) == 1:
            own[...] = own[...] + others[0][...]
            line.busy(ADD_US)
            return
        total = own[...].astype(F32)
        for other in others:
            total += other[...].astype(F32)
        own[...] = total.astype(own.dtype)
        line.busy(ADD_US)

    def ring(axis, view, d, halves, fulls):
        slot = FAR_FIRST.index(d)
        z = comm.step("z", d)
        left = comm.send(view(z, comm.step(axis, 2), 0), halves.at[slot, 0], axis, 1)
        right = comm.send(view(z, comm.step(axis, 2), 1), halves.at[slot, 1], axis, -1)
        yield [left]
        left()
        add(view(z, comm.step(axis, 1), 0), halves.at[slot, 0])
        left = comm.send(view(z, comm.step(axis, 1)), fulls.at[slot, 0], axis, 1)
        yield [right]
        right()
        add(view(z, comm.step(axis, -1), 1), halves.at[slot, 1])
        right = comm.send(view(z, comm.step(axis, -1)), fulls.at[slot, 1], axis, -1)
        yield [left, right]
        left()
        right()
        add(view(z, comm.at(axis)), fulls.at[slot, 0], fulls.at[slot, 1])

    def side(rings, cut, bufs):
        (near, single), (wide, four) = rings
        landing = bufs[4]
        waits = []
        gate = Event()
        left = [8]

        def chain(d):
            yield ready[d]
            yield from ring(wide, four, d, bufs[0], bufs[1])
            yield from ring(near, single, d, bufs[2], bufs[3])
            if d:
                waits.append(
                    comm.send(single(comm.step("z", d), comm.at(near)), landing.at[len(waits)], "z", d)
                )
            left[0] -= 1
            if left[0] == 0:
                line.fire(gate)

        def rest():
            yield gate
            yield list(waits)
            for wait in waits:
                wait()
            total = single(comm.z, comm.at(near))[...].astype(F32)
            for i in range(7):
                total += landing[i].astype(F32)
            result[cut[0] : cut[1]] = total
            line.busy(ADD_US)

        for d in FAR_FIRST:
            line.spawn(chain(d))
        line.spawn(rest())

    views = ring_views(comm, partial)
    third = third_view(comm, partial)
    halves, fulls, landing, row, last = buffers[10:15]
    waits = []

    def along_z(slot, o):
        y = comm.step("y", o)
        yield ready[4]
        left = comm.send(third(comm.step("z", 4), y, 0), halves.at[slot, 0], "z", 1)
        right = comm.send(third(comm.step("z", 4), y, 1), halves.at[slot, 1], "z", -1)
        came = (halves.at[slot, 0], halves.at[slot, 1])
        for s in (3, 2, 1):
            yield ready[s]
            yield [left]
            left()
            add(third(comm.step("z", s), y, 0 if s == 3 else None), came[0])
            left = comm.send(third(comm.step("z", s), y), fulls.at[slot, s - 1, 0], "z", 1)
            yield ready[-s]
            yield [right]
            right()
            add(third(comm.step("z", -s), y, 1 if s == 3 else None), came[1])
            right = comm.send(third(comm.step("z", -s), y), fulls.at[slot, s - 1, 1], "z", -1)
            came = (fulls.at[slot, s - 1, 0], fulls.at[slot, s - 1, 1])
        yield ready[0]
        yield [left, right]
        left()
        right()
        mine = third(comm.z, y)
        if o:
            add(mine, *came)
            waits.append(comm.send(mine, landing.at[slot], "y", o))
        else:
            row[...] = mine[...].astype(F32) + came[0][...].astype(F32) + came[1][...].astype(F32)
            line.busy(ADD_US)

    gate = Event()
    pending = [4]

    def one(slot, o):
        yield from along_z(slot, o)
        pending[0] -= 1
        if pending[0] == 0:
            line.fire(gate)

    def rest():
        yield gate
        yield list(waits)
        for wait in waits:
            wait()
        total = row[...]
        for i in range(3):
            total += landing[i].astype(F32)
        row[...] = total
        line.busy(ADD_US)
        ends = [comm.send(row.at[comm.step("x", o)], last.at[k], "x", o) for k, o in enumerate((1, -1, 2))]
        yield ends
        for wait in ends:
            wait()
        result[CUTS[2][0] : CUTS[2][1]] = row[comm.x] + last[0] + last[1] + last[2]

    for slot, o in enumerate((2, 1, -1, 0)):
        line.spawn(one(slot, o))
    side(views[0], CUTS[0], buffers[0:5])
    side(views[1], CUTS[1], buffers[5:10])
    line.spawn(rest())


def load_hidden(held, z):
    tiles = []
    for pair in (0, 1):
        even, odd = 2 * pair, 2 * pair + 1
        middle = jnp.concatenate([held[z, even, :, :, 7:11], held[z, odd, :, :, 0:3]], axis=2)
        for part in (held[z, even, :, :, 0:7], middle, held[z, odd, :, :, 3:10]):
            tiles.append(part.reshape(TOK, LANES))
    return jnp.concatenate(tiles, axis=1)


def selection(odd):
    feature = lax.broadcasted_iota(jnp.int32, (WIDE, 2 * LANES), 0)
    place = lax.broadcasted_iota(jnp.int32, (WIDE, 2 * LANES), 1)
    return (place == feature + 40 * odd).astype(F32).astype(BF16)


def kernel(
    pair_ref, ref_ref, own_ref, weight_ref, target_ref, mask_ref,
    logprobs_ref, hidden_grad_ref, weight_grad_ref,
    held, partial, padded, logits, dlogits, shared_out, shared_in, stats, far, near, final, near_out, swapped,
    send_sem, recv_sem, local_sem, *buffers,
):
    comm = Comm(send_sem, recv_sem)
    odd = lax.rem(comm.y, 2)
    even = odd == 0

    barrier = pltpu.get_barrier_semaphore()
    peers = []
    for axis, n in (("section", 8), ("tensor", 4), ("dp", 8)):
        me = lax.axis_index(axis)
        for offset in range(1, n):
            place = {"section": comm.z, "tensor": comm.y, "dp": comm.dp}
            place[axis] = lax.rem(me + offset, n)
            peers.append((place["section"], place["tensor"], place["dp"]))
    for peer in peers:
        pl.semaphore_signal(barrier, inc=1, device_id=peer, device_id_type=MESH)

    def weight_copy(i):
        return pltpu.make_async_copy(
            weight_ref.at[pl.ds(pl.multiple_of(i * PAIR, TILE), PAIR)],
            padded.at[pl.ds(pl.multiple_of(i * PADDED, TILE), PAIR)],
            local_sem.at[i],
        )

    for i in range(PAIRS):
        weight_copy(i).start()

    spread = lax.dot_general(
        own_ref[...], selection(odd), (((0,), (0,)), ((), ())), preferred_element_type=F32
    ).astype(BF16)
    low, high = spread[:, :LANES], spread[:, LANES:]
    alone = jnp.where(even, low, high).reshape(7, TILE, LANES)
    shared_out[...] = jnp.where(even, high, low).reshape(7, TILE, LANES)
    pl.semaphore_wait(barrier, len(peers))

    wait = comm.send(shared_out, shared_in, comm.partner())
    for i in range(PAIRS):
        padded[i * PADDED + PAIR : (i + 1) * PADDED] = jnp.zeros((PADDED - PAIR, COLS), BF16)
    logits[...] = jnp.zeros_like(logits)
    wait()
    shared = shared_out[...] + shared_in[...]
    zero_tile = jnp.zeros((1, TILE, LANES), BF16)
    held[comm.z, comm.y, comm.x, comm.c] = jnp.where(
        even,
        jnp.concatenate([alone, shared[0:4]], axis=0),
        jnp.concatenate([shared[4:7], alone, zero_tile], axis=0),
    )

    def add_logits(z, d):
        if d == 0:
            for i in range(PAIRS):
                weight_copy(i).wait()
        logits[...] += jnp.dot(
            load_hidden(held, z),
            padded[pl.ds(pl.multiple_of(z * 2 * PADDED, LANES), 2 * PADDED)],
            preferred_element_type=F32,
        )

    line = comm.line
    gather(comm, held, line, add_logits)

    def column(row):
        return jnp.broadcast_to(row, (LANES, LANES)).T[:, 0:1]

    def target_column(j):
        return column(target_ref[j : j + 1].astype(F32))

    first = ((comm.z * 4 + comm.y) * 8 + comm.dp) * COLS
    columns = first + lax.broadcasted_iota(jnp.int32, (LANES, COLS), 1)
    columns = columns.astype(F32)
    lane = lax.broadcasted_iota(jnp.int32, (LANES, LANES), 1)
    stats[...] = jnp.zeros_like(stats)
    for j in range(TOK // LANES):
        rows = slice(j * LANES, (j + 1) * LANES)
        block = logits[rows]
        top = jnp.max(block, axis=1, keepdims=True)
        total = jnp.sum(jnp.exp(block - top), axis=1, keepdims=True)
        picked = jnp.sum(jnp.where(target_column(j) == columns, block, 0.0), axis=1, keepdims=True)
        turned = jnp.where(lane == 0, top + jnp.log(total), picked).T
        for i in range(2):
            stats[i, j : j + 1] = turned[i : i + 1]

    for axis, n, slots in (("dp", 8, far.at[0]), ("tensor", 4, near), ("section", 8, far.at[1])):
        me = lax.axis_index(axis)
        waits = []
        slots[me] = stats[...]
        for offset in range(1, n):
            place = {"section": comm.z, "tensor": comm.y, "dp": comm.dp}
            place[axis] = lax.rem(me + offset, n)
            waits.append(
                comm.send(
                    slots.at[me],
                    slots.at[me],
                    (place["section"], place["tensor"], place["dp"]),
                    landing=slots.at[lax.rem(me + n - offset, n)],
                )
            )
        for wait in waits:
            wait()
        tops = [slots[i, 0] for i in range(n)]
        top = tops[0]
        for i in range(1, n):
            top = jnp.maximum(top, tops[i])
        total = jnp.exp(tops[0] - top)
        picked = slots[0, 1]
        for i in range(1, n):
            total += jnp.exp(tops[i] - top)
            picked += slots[i, 1]
        stats[0] = top + jnp.log(total)
        stats[1] = picked
        comm.drain()

    log_total = stats[0]
    terms = stats[1] - log_total

    def flat(rows):
        return jnp.concatenate([rows[j : j + 1] for j in range(TOK // LANES)], axis=1)

    token = lax.broadcasted_iota(jnp.int32, (SEQS, TOK), 1)
    start = SEQ * lax.broadcasted_iota(jnp.int32, (SEQS, TOK), 0)
    onehot = jnp.where((token >= start) & (token < start + SEQ), flat(mask_ref[...].astype(F32)), 0.0)
    counts = jnp.sum(onehot, axis=1, keepdims=True)
    seq = (SEQS, SEQS)
    down, right = lax.broadcasted_iota(jnp.int32, seq, 0), lax.broadcasted_iota(jnp.int32, seq, 1)
    pair_down, pair_right = jnp.zeros(seq, jnp.int32), jnp.zeros(seq, jnp.int32)
    ref_down = jnp.zeros(seq, F32)
    for i in range(SEQS):
        pair_down = jnp.where(down == i, pair_ref[i], pair_down)
        pair_right = jnp.where(right == i, pair_ref[i], pair_right)
        ref_down = jnp.where(down == i, ref_ref[i], ref_down)
    same = jnp.where(pair_down == pair_right, 1.0, 0.0)
    earlier = jnp.sum(jnp.where(right < down, same, 0.0), axis=1, keepdims=True)
    sign = jnp.where(earlier == 0.0, 1.0, -1.0)
    eye = down == right

    logprobs = jnp.sum(onehot * flat(terms), axis=1, keepdims=True) / counts
    logprobs_ref[...] = jnp.sum(jnp.where(eye, logprobs, 0.0), axis=0, keepdims=True)
    contrib = sign * (logprobs - ref_down[:, 0:1])
    across = jnp.sum(jnp.where(eye, contrib, 0.0), axis=0, keepdims=True)
    margin = jnp.sum(same * across, axis=1, keepdims=True)
    coefficient = -loss_scale * beta_value * jax.nn.sigmoid(-beta_value * margin) * sign
    token_weight = jnp.sum(onehot * (coefficient / counts), axis=0, keepdims=True)

    for j in range(TOK // LANES):
        rows = slice(j * LANES, (j + 1) * LANES)
        probs = jnp.exp(logits[rows] - column(log_total[j : j + 1]))
        hit = (target_column(j) == columns).astype(F32)
        dlogits[rows] = (column(token_weight[:, rows]) * (hit - probs)).astype(BF16)

    line = comm.line
    ready = {d: Event() for d in FAR_FIRST}

    def hidden_grad(d):
        z = comm.step("z", d)
        for pair in (0, 1):
            terms = lax.dot_general(
                dlogits[...],
                padded[pl.ds(pl.multiple_of((2 * z + pair) * PADDED, LANES), PADDED)],
                (((1,), (1,)), ((), ())),
                preferred_element_type=F32,
            ).astype(BF16)
            left, middle, right = (
                terms[:, i * LANES : (i + 1) * LANES].reshape(4, 2, 7, TILE, LANES) for i in range(3)
            )
            partial[z, 2 * pair, :, :, 0:7] = left
            partial[z, 2 * pair, :, :, 7:11] = middle[:, :, 0:4]
            partial[z, 2 * pair + 1, :, :, 0:3] = middle[:, :, 4:7]
            partial[z, 2 * pair + 1, :, :, 3:10] = right
            partial[z, 2 * pair + 1, :, :, 10:11] = jnp.zeros((4, 2, 1, TILE, LANES), BF16)
        wait = comm.send(partial.at[z, :, :, 1 - comm.c], near_out.at[FAR_FIRST.index(d)], "c", 1)

        def rest():
            yield [wait]
            wait()
            for y in range(4):
                partial[z, y, :, comm.c] = partial[z, y, :, comm.c] + near_out[FAR_FIRST.index(d), y]
            line.busy(ADD_US)
            line.fire(ready[d])

        line.spawn(rest())

    def grad_copy(i):
        return pltpu.make_async_copy(
            padded.at[pl.ds(pl.multiple_of(i * PADDED, TILE), PAIR)],
            weight_grad_ref.at[pl.ds(pl.multiple_of(i * PAIR, TILE), PAIR)],
            local_sem.at[i],
        )

    def weight_grad(z):
        def item():
            block = lax.dot_general(
                load_hidden(held, z), dlogits[...], (((0,), (0,)), ((), ())), preferred_element_type=F32
            )
            padded[z * 2 * PADDED : (z + 1) * 2 * PADDED] = block.astype(BF16)
            grad_copy(2 * z).start()
            grad_copy(2 * z + 1).start()

        return item

    def compute():
        for d in FAR_FIRST:
            hidden_grad(d)
            line.busy(MATMUL_US)
            yield []
        line.work = [weight_grad(z) for z in range(8)]

    line.spawn(compute())
    reduce(comm, partial, final, buffers, line, ready)
    line.run()

    mine = final[...].astype(BF16)
    comm.drain()
    shared_out[0:4] = jnp.where(even, mine[7:11], jnp.concatenate([mine[0:3], mine[0:1]], axis=0))
    comm.send(shared_out.at[0:4], swapped, comm.partner())()
    other = swapped[...]
    alone = jnp.where(even, mine[0:7], mine[3:10]).reshape(ROWS, LANES)
    shared = jnp.where(
        even,
        jnp.concatenate([mine[7:11], other[0:3]], axis=0),
        jnp.concatenate([other, mine[0:3]], axis=0),
    ).reshape(ROWS, LANES)
    both = jnp.concatenate([jnp.where(even, alone, shared), jnp.where(even, shared, alone)], axis=1)
    hidden_grad_ref[...] = lax.dot_general(
        selection(odd), both, (((1,), (1,)), ((), ())), preferred_element_type=F32
    ).astype(BF16)
    comm.drain()
    for i in range(PAIRS):
        grad_copy(i).wait()


def per_device(hidden, head_weight, targets, response_mask, pair_ids, ref_logprobs):
    vmem = pl.BlockSpec(memory_space=pltpu.VMEM)
    smem = pl.BlockSpec(memory_space=pltpu.SMEM)
    hbm = pl.BlockSpec(memory_space=pl.ANY)
    copies = 400
    logprobs, turned, grad_weight = pl.pallas_call(
        kernel,
        out_shape=(
            jax.ShapeDtypeStruct((1, SEQS), F32),
            jax.ShapeDtypeStruct((WIDE, ROWS), BF16),
            jax.ShapeDtypeStruct(head_weight.shape, BF16),
        ),
        in_specs=[smem, smem, vmem, hbm, vmem, vmem],
        out_specs=(vmem, vmem, hbm),
        scratch_shapes=[
            pltpu.VMEM((8, 4, 4, 2, BLOB, TILE, LANES), BF16),
            pltpu.VMEM((8, 4, 4, 2, BLOB, TILE, LANES), BF16),
            pltpu.VMEM((PAIRS * PADDED, COLS), BF16),
            pltpu.VMEM((TOK, COLS), F32),
            pltpu.VMEM((TOK, COLS), BF16),
            pltpu.VMEM((7, TILE, LANES), BF16),
            pltpu.VMEM((7, TILE, LANES), BF16),
            pltpu.VMEM((2, 8, LANES), F32),
            pltpu.VMEM((2, 8, 2, 8, LANES), F32),
            pltpu.VMEM((4, 2, 8, LANES), F32),
            pltpu.VMEM((BLOB, TILE, LANES), F32),
            pltpu.VMEM((8, 4, 4, BLOB, TILE, LANES), BF16),
            pltpu.VMEM((4, TILE, LANES), BF16),
            pltpu.SemaphoreType.DMA((copies,)),
            pltpu.SemaphoreType.DMA((copies,)),
            pltpu.SemaphoreType.DMA((PAIRS,)),
            *reduce_shapes(),
        ],
        compiler_params=pltpu.CompilerParams(
            collective_id=0, has_side_effects=True, vmem_limit_bytes=50 * 1024 * 1024
        ),
        cost_estimate=pl.CostEstimate(
            flops=6 * TOK * 5376 * COLS, bytes_accessed=12 * 1024 * 1024, transcendentals=2 * TOK * COLS
        ),
    )(
        pair_ids, ref_logprobs, hidden.T, head_weight,
        targets.reshape(TOK // LANES, LANES), response_mask.reshape(TOK // LANES, LANES),
    )
    return (logprobs.reshape(SEQS), turned.T, grad_weight)


def solution(mesh):
    placed = (
        P("dp", ("section", "tensor")),
        P(None, ("section", "tensor", "dp")),
        P(),
        P(),
        P(),
        P(),
    )
    return jax.shard_map(
        per_device,
        mesh=mesh,
        in_specs=placed,
        out_specs=(P(), P("dp", ("section", "tensor")), P(None, ("section", "tensor", "dp"))),
        check_vma=False,
    )
```

profile of v0, /device:TPU:8, one launch (start us, length us, event | category | flops | bytes accessed | tf_op | source)
XLA Modules:
  0.0 121.9 jit_solution(4344540264295926587)
XLA Ops:
  0.6 0.0 copy-start
  0.6 0.8 copy-done
  1.4 0.0 copy-start.1
  1.4 0.7 copy-done.1
  2.1 0.0 copy-start.2
  2.1 0.7 copy-done.2
  2.8 0.0 copy-start.3
  2.8 0.7 copy-done.3
  3.4 0.0 copy-start.4
  3.4 0.7 copy-done.4
  4.1 111.3 %shard_map.85 = (f32[1,16]{1,0:T(1,128)S(1)}, bf16[168,112]{1,0:T(8,128)(2,1)S(1)}, bf16[5376,512]{1,0:T(8,128)(2,1)}) custom-call(s32[16]{0:T(128)S(1)} %copy-done.3, f32[16]{0:T(128)S(1)} %copy-done.4, bf16[168,112]{1,0:T(8,128)(2,1)S(1)} %bitcast.6, bf16[5376,512]{1,0:T(8,128)(2,1)} %weight_ref.1, s32[7,128]{1,0:T(8,128)S(1)} %bitcast.7, s32[7,128]{1,0:T(8,128)S(1)} %bitcast.8), custom_call_target="tpu_custom_call" | custom-call | flops 14797504512 | bytes 12582912 | tf_op jit(solution)/shard_map/pallas_call | solution.py:735
  115.4 0.5 copy.12
  115.9 0.6 copy.13
  116.5 5.4 %copy.14 = bf16[5376,512]{1,0:T(8,128)(2,1)} copy(bf16[5376,512]{1,0:T(8,128)(2,1)} %get-tuple-element.14) | data formatting | bytes 11010048
Async XLA Ops:
  0.6 0.8 copy-start
  1.4 0.7 copy-start.1
  2.1 0.7 copy-start.2
  2.8 0.7 copy-start.3
  3.4 0.7 copy-start.4
where the time goes:
time: 122 us
  Pallas kernels  111 us (91%)
  local copies, waits for them, and re-layouts  9.95 us (8%)
    pallas_call x1, Pallas kernels, per_device(): pl.pallas_call(kernel, out_shape=(jax.ShapeDtypeStruct((1, SEQS), F32), j...  111 us
    unnamed x13, local copies, waits for them, and re-layouts  9.95 us

commit v1 on v0

--- a/solution.py
+++ b/solution.py
@@ -15,6 +15,7 @@
 MESH = pl.DeviceIdType.MESH
 SIZE = {"z": 8, "y": 4, "x": 4}
 BLOB = 11
+OWN_TILES = 7
 CUTS = ((0, 4), (4, 8), (8, 11))
 LANES = 128
 TILE = 16
@@ -29,13 +30,13 @@
 PADDED = 384
 F32 = jnp.float32
 BF16 = jnp.bfloat16
-ISSUE_US = 0.05
+ISSUE_US = 0.02
 HOP_US = 1.5
 EACH_HOP_US = 0.5
 LINK = 45.0e3
 CORE_LINK = 600.0e3
 MATMUL_US = 0.8
-ADD_US = 0.06
+ADD_US = 0.03
 FAR_FIRST = (4, 3, -3, 2, -2, 1, -1, 0)
 
 
@@ -102,7 +103,8 @@
             device_id_type=MESH,
         )
         size = math.prod(src.shape) * jnp.dtype(src.dtype).itemsize
-        return Landing(self.line, back, self.line.now if offset is None else self.line.carry(axis, offset, size))
+        when = self.line.now + 2 * HOP_US if offset is None else self.line.carry(axis, offset, size)
+        return Landing(self.line, back, when)
 
     def drain(self):
         for copy in self.unsent:
@@ -213,24 +215,28 @@
     return view
 
 
-def gather(comm, held, line, add_logits):
+def gather(comm, held, line, add_logits, swap):
     place = (comm.z, comm.y, comm.x, comm.c)
-    missing = {d: 6 for d in FAR_FIRST}
-
-    def finish(d):
-        missing[d] -= 1
-        if missing[d] == 0:
-            z = comm.step("z", d)
-            src = held.at[z, :, :, comm.c]
-            wait = comm.send(src, src, "c", 1, landing=held.at[z, :, :, 1 - comm.c])
-
-            def rest():
-                yield [wait]
-                wait()
-                add_logits(z, d)
-                line.busy(MATMUL_US)
-
-            line.spawn(rest())
+    pieces = {d: [1, 1, 4] for d in FAR_FIRST}
+    other = {d: [] for d in FAR_FIRST}
+
+    def finish(part, d):
+        pieces[d][part] -= 1
+        if pieces[d][part]:
+            return
+        z = comm.step("z", d)
+        cut = slice(*CUTS[part])
+        src = held.at[z, :, :, comm.c, cut]
+        other[d].append(comm.send(src, src, "c", 1, landing=held.at[z, :, :, 1 - comm.c, cut]))
+        if len(other[d]) == 3:
+            line.spawn(rest(z, d))
+
+    def rest(z, d):
+        yield other[d]
+        for wait in other[d]:
+            wait()
+        add_logits(z, d)
+        line.busy(MATMUL_US)
 
     def ring(axis, view, d):
         z = comm.step("z", d)
@@ -249,22 +255,27 @@
         left()
         right()
 
-    def chain(rings, d, wait=None):
-        if wait is not None:
-            yield [wait]
-            wait()
-        for axis, view in rings:
+    def chain(part, d):
+        for axis, view in views[part]:
             yield from ring(axis, view, d)
-        finish(d)
+        finish(part, d)
 
     views = ring_views(comm, held)
-    first = slice(CUTS[0][0], CUTS[1][1])
+    joined = slice(OWN_TILES, CUTS[1][1])
+    first = slice(0, OWN_TILES)
+    here = {d: Event() for d in FAR_FIRST}
 
     def arrive(d, wait):
         yield [wait]
         wait()
-        for rings in views:
-            line.spawn(chain(rings, d))
+        line.spawn(chain(0, d))
+        yield here[d]
+        line.spawn(chain(1, d))
+
+    def arrive_joined(d, wait):
+        yield [wait]
+        wait()
+        line.fire(here[d])
 
     def along_z(y):
         third = third_view(comm, held)
@@ -275,14 +286,14 @@
             src = third(comm.step("z", s - 1), y, h1)
             right = comm.send(src, src, "z", -1, landing=third(comm.step("z", s), y, h1))
             if s == 1:
-                finish(0)
+                finish(2, 0)
             yield [left, right]
             left()
             right()
             if s < 4:
-                finish(-s)
-                finish(s)
-        finish(4)
+                finish(2, -s)
+                finish(2, s)
+        finish(2, 4)
 
     def start_third():
         lo, hi = CUTS[2]
@@ -307,20 +318,28 @@
             wait()
             line.spawn(along_z(comm.step("y", -o)))
 
-    line.spawn(start_third())
-    for rings in views:
-        line.spawn(chain(rings, 0))
-
-    def spread():
-        src = held.at[(*place, first)]
+    def spread(tiles, then):
+        src = held.at[(*place, tiles)]
         for o in NEAR_FIRST:
-            landing = held.at[comm.step("z", -o), comm.y, comm.x, comm.c, first]
+            landing = held.at[comm.step("z", -o), comm.y, comm.x, comm.c, tiles]
             wait = comm.send(src, src, "z", o, landing=landing)
-            line.spawn(arrive(4 if o == 4 else -o, wait))
+            line.spawn(then(4 if o == 4 else -o, wait))
+
+    def start():
+        yield from swap()
+        line.spawn(start_third())
+        line.spawn(chain(1, 0))
+        spread(joined, arrive_joined)
+
+    line.spawn(start())
+    line.spawn(chain(0, 0))
+
+    def begin():
+        spread(first, arrive)
         return
         yield
 
-    line.spawn(spread())
+    line.spawn(begin())
     line.run()
 
 
@@ -346,7 +365,7 @@
     return shapes
 
 
-def reduce(comm, partial, result, buffers, line, ready):
+def reduce(comm, partial, result, buffers, line, ready, shared_done):
     def add(own, *others):
         if len(others) == 1:
             own[...] = own[...] + others[0][...]
@@ -405,6 +424,8 @@
                 total += landing[i].astype(F32)
             result[cut[0] : cut[1]] = total
             line.busy(ADD_US)
+            if cut == CUTS[1]:
+                line.fire(shared_done[0])
 
         for d in FAR_FIRST:
             line.spawn(chain(d))
@@ -469,6 +490,7 @@
         for wait in ends:
             wait()
         result[CUTS[2][0] : CUTS[2][1]] = row[comm.x] + last[0] + last[1] + last[2]
+        line.fire(shared_done[1])
 
     for slot, o in enumerate((2, 1, -1, 0)):
         line.spawn(one(slot, o))
@@ -481,8 +503,8 @@
     tiles = []
     for pair in (0, 1):
         even, odd = 2 * pair, 2 * pair + 1
-        middle = jnp.concatenate([held[z, even, :, :, 7:11], held[z, odd, :, :, 0:3]], axis=2)
-        for part in (held[z, even, :, :, 0:7], middle, held[z, odd, :, :, 3:10]):
+        middle = jnp.concatenate([held[z, even, :, :, 7:11], held[z, odd, :, :, 7:10]], axis=2)
+        for part in (held[z, even, :, :, 0:7], middle, held[z, odd, :, :, 0:7]):
             tiles.append(part.reshape(TOK, LANES))
     return jnp.concatenate(tiles, axis=1)
 
@@ -532,18 +554,21 @@
     shared_out[...] = jnp.where(even, high, low).reshape(7, TILE, LANES)
     pl.semaphore_wait(barrier, len(peers))
 
-    wait = comm.send(shared_out, shared_in, comm.partner())
-    for i in range(PAIRS):
-        padded[i * PADDED + PAIR : (i + 1) * PADDED] = jnp.zeros((PADDED - PAIR, COLS), BF16)
-    logits[...] = jnp.zeros_like(logits)
-    wait()
-    shared = shared_out[...] + shared_in[...]
-    zero_tile = jnp.zeros((1, TILE, LANES), BF16)
-    held[comm.z, comm.y, comm.x, comm.c] = jnp.where(
-        even,
-        jnp.concatenate([alone, shared[0:4]], axis=0),
-        jnp.concatenate([shared[4:7], alone, zero_tile], axis=0),
-    )
+    held[comm.z, comm.y, comm.x, comm.c, 0:OWN_TILES] = alone
+
+    def swap():
+        wait = comm.send(shared_out, shared_in, comm.partner())
+        for i in range(PAIRS):
+            padded[i * PADDED + PAIR : (i + 1) * PADDED] = jnp.zeros((PADDED - PAIR, COLS), BF16)
+        logits[...] = jnp.zeros_like(logits)
+        yield [wait]
+        wait()
+        shared = shared_out[...] + shared_in[...]
+        held[comm.z, comm.y, comm.x, comm.c, OWN_TILES:BLOB] = jnp.where(
+            even,
+            shared[0:4],
+            jnp.concatenate([shared[4:7], jnp.zeros((1, TILE, LANES), BF16)], axis=0),
+        )
 
     def add_logits(z, d):
         if d == 0:
@@ -556,7 +581,7 @@
         )
 
     line = comm.line
-    gather(comm, held, line, add_logits)
+    gather(comm, held, line, add_logits, swap)
 
     def column(row):
         return jnp.broadcast_to(row, (LANES, LANES)).T[:, 0:1]
@@ -663,8 +688,8 @@
             )
             partial[z, 2 * pair, :, :, 0:7] = left
             partial[z, 2 * pair, :, :, 7:11] = middle[:, :, 0:4]
-            partial[z, 2 * pair + 1, :, :, 0:3] = middle[:, :, 4:7]
-            partial[z, 2 * pair + 1, :, :, 3:10] = right
+            partial[z, 2 * pair + 1, :, :, 0:7] = right
+            partial[z, 2 * pair + 1, :, :, 7:10] = middle[:, :, 4:7]
             partial[z, 2 * pair + 1, :, :, 10:11] = jnp.zeros((4, 2, 1, TILE, LANES), BF16)
         wait = comm.send(partial.at[z, :, :, 1 - comm.c], near_out.at[FAR_FIRST.index(d)], "c", 1)
 
@@ -703,20 +728,27 @@
             yield []
         line.work = [weight_grad(z) for z in range(8)]
 
+    shared_done = (Event(), Event())
+
+    def swap_back():
+        yield shared_done[0]
+        yield shared_done[1]
+        shared_out[0:4] = final[OWN_TILES:BLOB].astype(BF16)
+        wait = comm.send(shared_out.at[0:4], swapped, comm.partner())
+        yield [wait]
+        wait()
+
     line.spawn(compute())
-    reduce(comm, partial, final, buffers, line, ready)
+    line.spawn(swap_back())
+    reduce(comm, partial, final, buffers, line, ready, shared_done)
     line.run()
 
-    mine = final[...].astype(BF16)
-    comm.drain()
-    shared_out[0:4] = jnp.where(even, mine[7:11], jnp.concatenate([mine[0:3], mine[0:1]], axis=0))
-    comm.send(shared_out.at[0:4], swapped, comm.partner())()
-    other = swapped[...]
-    alone = jnp.where(even, mine[0:7], mine[3:10]).reshape(ROWS, LANES)
+    mine, other = final[...].astype(BF16), swapped[...]
+    alone = mine[0:OWN_TILES].reshape(ROWS, LANES)
     shared = jnp.where(
         even,
         jnp.concatenate([mine[7:11], other[0:3]], axis=0),
-        jnp.concatenate([other, mine[0:3]], axis=0),
+        jnp.concatenate([other, mine[7:10]], axis=0),
     ).reshape(ROWS, LANES)
     both = jnp.concatenate([jnp.where(even, alone, shared), jnp.where(even, shared, alone)], axis=1)
     hidden_grad_ref[...] = lax.dot_general(
@@ -727,11 +759,33 @@
         grad_copy(i).wait()
 
 
+def move(logprobs_ref, turned_ref, source, logprobs_out, turned_out, result, block, in_sems, out_sems):
+    rows = source.shape[0] // PAIRS
+    pieces = [pl.ds(i * rows, rows) for i in range(PAIRS)]
+    reads = [
+        pltpu.make_async_copy(source.at[piece], block.at[piece], in_sems.at[i])
+        for i, piece in enumerate(pieces)
+    ]
+    writes = [
+        pltpu.make_async_copy(block.at[piece], result.at[piece], out_sems.at[i])
+        for i, piece in enumerate(pieces)
+    ]
+    for read in reads:
+        read.start()
+    logprobs_out[...] = logprobs_ref[...]
+    turned_out[...] = turned_ref[...]
+    for read, write in zip(reads, writes):
+        read.wait()
+        write.start()
+    for write in writes:
+        write.wait()
+
+
 def per_device(hidden, head_weight, targets, response_mask, pair_ids, ref_logprobs):
     vmem = pl.BlockSpec(memory_space=pltpu.VMEM)
     smem = pl.BlockSpec(memory_space=pltpu.SMEM)
     hbm = pl.BlockSpec(memory_space=pl.ANY)
-    copies = 400
+    copies = 448
     logprobs, turned, grad_weight = pl.pallas_call(
         kernel,
         out_shape=(
@@ -761,7 +815,7 @@
             *reduce_shapes(),
         ],
         compiler_params=pltpu.CompilerParams(
-            collective_id=0, has_side_effects=True, vmem_limit_bytes=50 * 1024 * 1024
+            collective_id=0, has_side_effects=True, vmem_limit_bytes=60 * 1024 * 1024
         ),
         cost_estimate=pl.CostEstimate(
             flops=6 * TOK * 5376 * COLS, bytes_accessed=12 * 1024 * 1024, transcendentals=2 * TOK * COLS
@@ -770,6 +824,22 @@
         pair_ids, ref_logprobs, hidden.T, head_weight,
         targets.reshape(TOK // LANES, LANES), response_mask.reshape(TOK // LANES, LANES),
     )
+    logprobs, turned, grad_weight = pl.pallas_call(
+        move,
+        out_shape=(
+            jax.ShapeDtypeStruct((1, SEQS), F32),
+            jax.ShapeDtypeStruct((WIDE, ROWS), BF16),
+            jax.ShapeDtypeStruct(head_weight.shape, BF16),
+        ),
+        in_specs=[vmem, vmem, hbm],
+        out_specs=(vmem, vmem, hbm),
+        scratch_shapes=[
+            pltpu.VMEM(head_weight.shape, BF16),
+            pltpu.SemaphoreType.DMA((PAIRS,)),
+            pltpu.SemaphoreType.DMA((PAIRS,)),
+        ],
+        compiler_params=pltpu.CompilerParams(vmem_limit_bytes=60 * 1024 * 1024),
+    )(logprobs, turned, grad_weight)
     return (logprobs.reshape(SEQS), turned.T, grad_weight)
 
 

time: 122 us -> 119 us (0.975)
  local copies, waits for them, and re-layouts: 9.95 us -> 0 us
  Pallas kernels: 111 us -> 118 us
    unnamed x13 -> x0, local copies, waits for them, and re-layouts: 9.95 us -> none
    pallas_call x0 -> x1, Pallas kernels: none -> 6.52 us  [per_device(): pl.pallas_call(move, out_shape=(jax.ShapeDtypeStruct((1, SEQS), F32), jax...]
where the time goes in v1:
time: 119 us
  Pallas kernels  118 us (99%)
    pallas_call x1, Pallas kernels, per_device(): pl.pallas_call(kernel, out_shape=(jax.ShapeDtypeStruct((1, SEQS), F32), j...  112 us
    pallas_call x1, Pallas kernels, per_device(): pl.pallas_call(move, out_shape=(jax.ShapeDtypeStruct((1, SEQS), F32), jax...  6.52 us

profile of v1, /device:TPU:8, one launch (start us, length us, event | category | flops | bytes accessed | tf_op | source)
XLA Modules:
  0.0 119.2 jit_solution(3815963622977938435)
XLA Ops:
  0.6 111.9 %shard_map.85 = (f32[1,16]{1,0:T(1,128)}, bf16[168,112]{1,0:T(8,128)(2,1)}, bf16[5376,512]{1,0:T(8,128)(2,1)}) custom-call(s32[16]{0:T(128)} %pair_ref.1, f32[16]{0:T(128)} %ref_ref.1, bf16[168,112]{1,0:T(8,128)(2,1)} %bitcast.5, bf16[5376,512]{1,0:T(8,128)(2,1)} %weight_ref.1, s32[7,128]{1,0:T(8,128)} %bitcast.7, s32[7,128]{1,0:T(8,128)} %bitcast.8), custom_call_target="tpu_custom_call" | custom-call | flops 14797504512 | bytes 12582912 | tf_op jit(solution)/shard_map/pallas_call | solution.py:789
  112.5 6.5 %shard_map.86 = (f32[1,16]{1,0:T(1,128)}, bf16[168,112]{1,0:T(8,128)(2,1)}, bf16[5376,512]{1,0:T(8,128)(2,1)}) custom-call(f32[1,16]{1,0:T(1,128)} %get-tuple-element.9.logprobs_ref, bf16[168,112]{1,0:T(8,128)(2,1)} %get-tuple-element.10.turned_ref, bf16[5376,512]{1,0:T(8,128)(2,1)} %get-tuple-element.11.source), custom_call_target="tpu_custom_call" | custom-call | tf_op jit(solution)/shard_map/pallas_call | solution.py:827

commit v2 on v1

--- a/solution.py
+++ b/solution.py
@@ -180,7 +180,7 @@
             self.busy(MATMUL_US)
 
 
-NEAR_FIRST = (1, -1, 2, -2, 3, -3, 4)
+SPREAD = (2, -2, 1, -1, 3, -3, 4)
 
 
 def ring_views(comm, array):
@@ -320,7 +320,7 @@
 
     def spread(tiles, then):
         src = held.at[(*place, tiles)]
-        for o in NEAR_FIRST:
+        for o in SPREAD:
             landing = held.at[comm.step("z", -o), comm.y, comm.x, comm.c, tiles]
             wait = comm.send(src, src, "z", o, landing=landing)
             line.spawn(then(4 if o == 4 else -o, wait))
@@ -759,24 +759,18 @@
         grad_copy(i).wait()
 
 
-def move(logprobs_ref, turned_ref, source, logprobs_out, turned_out, result, block, in_sems, out_sems):
+def move(logprobs_ref, turned_ref, source, logprobs_out, turned_out, result, sems):
     rows = source.shape[0] // PAIRS
-    pieces = [pl.ds(i * rows, rows) for i in range(PAIRS)]
-    reads = [
-        pltpu.make_async_copy(source.at[piece], block.at[piece], in_sems.at[i])
-        for i, piece in enumerate(pieces)
+    writes = [
+        pltpu.make_async_copy(
+            source.at[pl.ds(i * rows, rows)], result.at[pl.ds(i * rows, rows)], sems.at[i]
+        )
+        for i in range(PAIRS)
     ]
-    writes = [
-        pltpu.make_async_copy(block.at[piece], result.at[piece], out_sems.at[i])
-        for i, piece in enumerate(pieces)
-    ]
-    for read in reads:
-        read.start()
+    for write in writes:
+        write.start()
     logprobs_out[...] = logprobs_ref[...]
     turned_out[...] = turned_ref[...]
-    for read, write in zip(reads, writes):
-        read.wait()
-        write.start()
     for write in writes:
         write.wait()
 
@@ -831,14 +825,12 @@
             jax.ShapeDtypeStruct((WIDE, ROWS), BF16),
             jax.ShapeDtypeStruct(head_weight.shape, BF16),
         ),
-        in_specs=[vmem, vmem, hbm],
+        in_specs=[vmem, vmem, vmem],
         out_specs=(vmem, vmem, hbm),
         scratch_shapes=[
-            pltpu.VMEM(head_weight.shape, BF16),
-            pltpu.SemaphoreType.DMA((PAIRS,)),
             pltpu.SemaphoreType.DMA((PAIRS,)),
         ],
-        compiler_params=pltpu.CompilerParams(vmem_limit_bytes=60 * 1024 * 1024),
+        compiler_params=pltpu.CompilerParams(vmem_limit_bytes=16 * 1024 * 1024),
     )(logprobs, turned, grad_weight)
     return (logprobs.reshape(SEQS), turned.T, grad_weight)
 

time: 119 us -> 119 us (level)
  local copies, waits for them, and re-layouts: 0 us -> 4.01 us
  Pallas kernels: 118 us -> 114 us
    unnamed x0 -> x6, local copies, waits for them, and re-layouts: none -> 4.01 us
    pallas_call x1, Pallas kernels: 6.52 us -> 3.17 us  [per_device(): pl.pallas_call(move, out_shape=(jax.ShapeDtypeStruct((1, SEQS), F32), jax...]
where the time goes in v2:
time: 119 us
  Pallas kernels  114 us (96%)
  local copies, waits for them, and re-layouts  4.01 us (3%)
    pallas_call x1, Pallas kernels, per_device(): pl.pallas_call(kernel, out_shape=(jax.ShapeDtypeStruct((1, SEQS), F32), j...  111 us
    unnamed x6, local copies, waits for them, and re-layouts  4.01 us
    pallas_call x1, Pallas kernels, per_device(): pl.pallas_call(move, out_shape=(jax.ShapeDtypeStruct((1, SEQS), F32), jax...  3.17 us

profile of v2, /device:TPU:8, one launch (start us, length us, event | category | flops | bytes accessed | tf_op | source)
XLA Modules:
  0.0 119.1 jit_solution(8411793979225672771)
XLA Ops:
  0.6 111.1 %shard_map.85 = (f32[1,16]{1,0:T(1,128)}, bf16[168,112]{1,0:T(8,128)(2,1)}, bf16[5376,512]{1,0:T(8,128)(2,1)}) custom-call(s32[16]{0:T(128)} %pair_ref.1, f32[16]{0:T(128)} %ref_ref.1, bf16[168,112]{1,0:T(8,128)(2,1)} %bitcast.5, bf16[5376,512]{1,0:T(8,128)(2,1)} %weight_ref.1, s32[7,128]{1,0:T(8,128)} %bitcast.7, s32[7,128]{1,0:T(8,128)} %bitcast.8), custom_call_target="tpu_custom_call" | custom-call | flops 14797504512 | bytes 12582912 | tf_op jit(solution)/shard_map/pallas_call | solution.py:783
  111.7 0.0 copy-start
  111.7 2.6 %copy-done = bf16[5376,512]{1,0:T(8,128)(2,1)S(1)} copy-done((bf16[5376,512]{1,0:T(8,128)(2,1)S(1)}, bf16[5376,512]{1,0:T(8,128)(2,1)}, u32[]{:S(2)}) %copy-start) | copy-done | bytes 5505048
  114.3 0.0 copy-start.1
  114.3 0.8 copy-done.1
  115.1 0.0 copy-start.2
  115.1 0.7 copy-done.2
  115.8 3.2 %shard_map.86 = (f32[1,16]{1,0:T(1,128)}, bf16[168,112]{1,0:T(8,128)(2,1)}, bf16[5376,512]{1,0:T(8,128)(2,1)}) custom-call(f32[1,16]{1,0:T(1,128)S(1)} %copy-done.2, bf16[168,112]{1,0:T(8,128)(2,1)S(1)} %copy-done.1, bf16[5376,512]{1,0:T(8,128)(2,1)S(1)} %copy-done), custom_call_target="tpu_custom_call" | custom-call | tf_op jit(solution)/shard_map/pallas_call | solution.py:821
Async XLA Ops:
  111.7 2.6 %copy-start = (bf16[5376,512]{1,0:T(8,128)(2,1)S(1)}, bf16[5376,512]{1,0:T(8,128)(2,1)}, u32[]{:S(2)}) copy-start(bf16[5376,512]{1,0:T(8,128)(2,1)} %get-tuple-element.11.source) | copy-start | bytes 16515076
  114.3 0.8 copy-start.1
  115.1 0.7 copy-start.2

commit v3 on v2

--- a/solution.py
+++ b/solution.py
@@ -181,6 +181,7 @@
 
 
 SPREAD = (2, -2, 1, -1, 3, -3, 4)
+GATHER_AT_ONCE = (0,)
 
 
 def ring_views(comm, array):
@@ -255,9 +256,20 @@
         left()
         right()
 
+    def at_once(axis, view, d):
+        z = comm.step("z", d)
+        src = view(z, comm.at(axis))
+        waits = [
+            comm.send(src, src, axis, o, landing=view(z, comm.step(axis, -o))) for o in (1, -1, 2)
+        ]
+        yield waits
+        for wait in waits:
+            wait()
+
     def chain(part, d):
-        for axis, view in views[part]:
-            yield from ring(axis, view, d)
+        near, far = views[part]
+        yield from (at_once if d in GATHER_AT_ONCE else ring)(*near, d)
+        yield from ring(*far, d)
         finish(part, d)
 
     views = ring_views(comm, held)

time: 119 us -> 118 us (level)
  no operation moved by 1% of the time
where the time goes in v3:
time: 118 us
  Pallas kernels  113 us (96%)
  local copies, waits for them, and re-layouts  4.01 us (3%)
    pallas_call x1, Pallas kernels, per_device(): pl.pallas_call(kernel, out_shape=(jax.ShapeDtypeStruct((1, SEQS), F32), j...  110 us
    unnamed x6, local copies, waits for them, and re-layouts  4.01 us
    pallas_call x1, Pallas kernels, per_device(): pl.pallas_call(move, out_shape=(jax.ShapeDtypeStruct((1, SEQS), F32), jax...  3.17 us

profile of v3, /device:TPU:8, one launch (start us, length us, event | category | flops | bytes accessed | tf_op | source)
XLA Modules:
  0.0 118.1 jit_solution(523845891716049095)
XLA Ops:
  0.6 110.1 %shard_map.85 = (f32[1,16]{1,0:T(1,128)}, bf16[168,112]{1,0:T(8,128)(2,1)}, bf16[5376,512]{1,0:T(8,128)(2,1)}) custom-call(s32[16]{0:T(128)} %pair_ref.1, f32[16]{0:T(128)} %ref_ref.1, bf16[168,112]{1,0:T(8,128)(2,1)} %bitcast.5, bf16[5376,512]{1,0:T(8,128)(2,1)} %weight_ref.1, s32[7,128]{1,0:T(8,128)} %bitcast.7, s32[7,128]{1,0:T(8,128)} %bitcast.8), custom_call_target="tpu_custom_call" | custom-call | flops 14797504512 | bytes 12582912 | tf_op jit(solution)/shard_map/pallas_call | solution.py:795
  110.7 0.0 copy-start
  110.7 2.6 %copy-done = bf16[5376,512]{1,0:T(8,128)(2,1)S(1)} copy-done((bf16[5376,512]{1,0:T(8,128)(2,1)S(1)}, bf16[5376,512]{1,0:T(8,128)(2,1)}, u32[]{:S(2)}) %copy-start) | copy-done | bytes 5505048
  113.3 0.0 copy-start.1
  113.3 0.8 copy-done.1
  114.1 0.0 copy-start.2
  114.1 0.7 copy-done.2
  114.8 3.2 %shard_map.86 = (f32[1,16]{1,0:T(1,128)}, bf16[168,112]{1,0:T(8,128)(2,1)}, bf16[5376,512]{1,0:T(8,128)(2,1)}) custom-call(f32[1,16]{1,0:T(1,128)S(1)} %copy-done.2, bf16[168,112]{1,0:T(8,128)(2,1)S(1)} %copy-done.1, bf16[5376,512]{1,0:T(8,128)(2,1)S(1)} %copy-done), custom_call_target="tpu_custom_call" | custom-call | tf_op jit(solution)/shard_map/pallas_call | solution.py:833
Async XLA Ops:
  110.7 2.6 %copy-start = (bf16[5376,512]{1,0:T(8,128)(2,1)S(1)}, bf16[5376,512]{1,0:T(8,128)(2,1)}, u32[]{:S(2)}) copy-start(bf16[5376,512]{1,0:T(8,128)(2,1)} %get-tuple-element.11.source) | copy-start | bytes 16515076
  113.3 0.8 copy-start.1
  114.1 0.7 copy-start.2
